TPU v7x, 32 devices: a whole 2x2x4 slice. The times are simulated.
32 devices in a mesh: groups: 2 (over y), pts: 4 (over z), cent: 4 (over x, core).
Axes of the slice: x: 2, y: 2, z: 4, core: 2. Of those that a mesh axis runs over, the one named last changes fastest.
Arguments:
- point_codes: bfloat16 [4096, 1024], P(('groups', 'pts')), parts along dimension 0, may hold values from -6 to 6
- shard_scales: float32 [16], P(('groups', 'pts')), parts along dimension 0, may hold values from 0.3 to 10
- coarse_centroids: bfloat16 [512, 1024], P('groups'), parts along dimension 0, may hold values from -1.5 to 1.5
- fine_centroids: bfloat16 [2048, 1024], P(('groups', 'pts'), 'cent'), parts along dimension 0, may hold values from -1.5 to 1.5
- block_lists: int32 [8, 16], P(('groups', 'pts')), parts along dimension 0, may hold values from 0 to 15, as said below
- live_counts: int32 [8], P(('groups', 'pts')), parts along dimension 0, may hold values from 1 to 16, as said below
Outputs:
- new_coarse: float32 [512, 1024], P(('groups', 'cent')), parts along dimension 0
- new_fine: float32 [2048, 1024], P(('groups', 'pts'), 'cent'), parts along dimension 0
There are 2 independent parts, one for each index of `groups`. A program takes and returns all parts, laid end to end along the dimension named above; each array names one. Nothing has to cross between parts.
Inputs may be any that keep to these rules, and one draw needn't show every extreme that they name: `block_lists`: within a row the entries are distinct, and at most 4 of them lie in any range q * 4 to q * 4 + 3; some such range holds 4 entries of every row, among them the first entry. Entries past the live count are valid block numbers too. Only the first live_counts[p] entries of row p of block_lists are used.
All inputs are finite; a program needn't handle non-finite values.
Results may differ from a plain program's by a relative error of at most 0.0028.
Values may be sent and summed in bfloat16 or wider, within the bound.
A program may use at most 64 MiB of HBM per device.

v0:
```python
import jax
import jax.numpy as jnp
from jax import lax
from jax.sharding import PartitionSpec as P

NCOARSE = 256
BLOCK = 64
SHARD = 256


PRIOR_MASS = 1.0
MASK_SCORE = -1e30


def joined(part, axis, combine):
    gathered = jax.tree.map(lambda a: lax.all_gather(a, axis), part)

    def take(source):
        return jax.tree.map(lambda a: lax.dynamic_index_in_dim(a, source, 0, False), gathered)

    return lax.fori_loop(
        1, lax.axis_size(axis), lambda source, state: combine(state, take(source)), take(0)
    )


def combine_norms(first_part, second_part):
    peak_value = jnp.maximum(first_part[0], second_part[0])
    scaled = first_part[1] * jnp.exp(first_part[0] - peak_value) + second_part[1] * jnp.exp(
        second_part[0] - peak_value
    )
    return (peak_value, scaled)


def rank_within(owner_ids):
    width_n = owner_ids.shape[-1]
    earlier_mask = jnp.arange(width_n)[None, :] < jnp.arange(width_n)[:, None]
    same_owner = owner_ids[..., :, None] == owner_ids[..., None, :]
    return jnp.sum(jnp.logical_and(same_owner, earlier_mask), axis=-1)


def owner_selection(owner_ids, local_index, chosen, pair_slots, own_blocks):
    rank_values = rank_within(owner_ids)
    by_rank = jnp.logical_and(
        chosen[..., None], rank_values[..., None] == jnp.arange(pair_slots)
    ).astype(jnp.float32)
    by_block = (local_index[..., None] == jnp.arange(own_blocks)).astype(jnp.float32)
    return jnp.einsum("psr,psl->prl", by_rank, by_block).reshape(-1, own_blocks)


def body(point_codes, shard_scales, coarse_centroids, fine_centroids, block_lists, live_counts):
    pts_count = lax.axis_size("pts")
    cent_count = lax.axis_size("cent")
    pts_index = lax.axis_index("pts")
    cent_index = lax.axis_index("cent")
    point_count, width_d = point_codes.shape
    own_blocks = fine_centroids.shape[0] // BLOCK
    quarter = fine_centroids.shape[1]
    capacity = block_lists.shape[1]
    my_slots = capacity // cent_count
    pair_slots = max(1, capacity // pts_count)
    row_scale = jnp.repeat(shard_scales, SHARD)
    all_lists = lax.all_gather(block_lists, "pts", axis=0, tiled=True)
    coarse_share = NCOARSE // cent_count
    coarse_mine = lax.dynamic_slice_in_dim(
        coarse_centroids, cent_index * coarse_share, coarse_share, 0
    )
    half_mine = 0.5 * jnp.sum(jnp.square(coarse_mine.astype(jnp.float32)), axis=1)
    coarse_score = (
        row_scale[:, None]
        * jnp.einsum("pd,kd->pk", point_codes, coarse_mine, preferred_element_type=jnp.float32)
        - half_mine[None, :]
    )
    local_peak = jnp.max(coarse_score, axis=1)
    local_total = jnp.sum(jnp.exp(coarse_score - local_peak[:, None]), axis=1)
    coarse_peak, coarse_total = joined((local_peak, local_total), "cent", combine_norms)
    coarse_resp = jnp.exp(coarse_score - coarse_peak[:, None]) / coarse_total[:, None]
    coarse_weight = (coarse_resp * row_scale[:, None]).astype(jnp.bfloat16)
    coarse_sum = jnp.einsum(
        "pk,pd->kd", coarse_weight, point_codes, preferred_element_type=jnp.float32
    )
    coarse_mass = jnp.sum(coarse_resp, axis=0)
    coarse_sum, coarse_mass = lax.psum((coarse_sum, coarse_mass), "pts")
    new_coarse = (coarse_sum + PRIOR_MASS * coarse_mine.astype(jnp.float32)) / (
        coarse_mass[:, None] + PRIOR_MASS
    )
    row_list = block_lists[0]
    row_owner = row_list // own_blocks
    row_position = row_owner * pair_slots + rank_within(row_owner)
    list_owner = all_lists // own_blocks
    list_local = all_lists % own_blocks
    return_picks = owner_selection(
        list_owner, list_local, list_owner == pts_index, pair_slots, own_blocks
    )
    my_start = cent_index * my_slots
    my_blocks = lax.dynamic_slice_in_dim(row_list, my_start, my_slots, 0)
    whole_rows = lax.all_gather(fine_centroids, "cent", axis=1, tiled=True)
    in_range = jnp.arange(capacity) // my_slots == cent_index
    owner_masked = jnp.where(in_range[None, :], list_owner, -1)
    selection = owner_selection(
        owner_masked, list_local, owner_masked == pts_index, pair_slots, own_blocks
    )
    outgoing = jnp.dot(
        selection.astype(jnp.bfloat16),
        whole_rows.reshape(own_blocks, BLOCK * width_d),
        preferred_element_type=jnp.bfloat16,
    )
    arrived = lax.all_to_all(
        outgoing.reshape(pts_count * pair_slots, BLOCK, width_d),
        "pts",
        split_axis=0,
        concat_axis=0,
        tiled=True,
    )
    my_owner = my_blocks // own_blocks
    my_position = my_owner * pair_slots + rank_within(my_owner)
    block_rows = jnp.take(arrived, my_position, axis=0)
    block_flat = block_rows.reshape(my_slots * BLOCK, width_d)
    half_fine = 0.5 * jnp.sum(jnp.square(block_flat.astype(jnp.float32)), axis=1).reshape(
        my_slots, BLOCK
    )
    fine_score = row_scale[:, None] * jnp.einsum(
        "pd,jd->pj", point_codes, block_flat, preferred_element_type=jnp.float32
    )
    fine_score = fine_score.reshape(point_count, my_slots, BLOCK) - half_fine[None]
    block_peak = jnp.max(fine_score, axis=2, keepdims=True)
    block_norm = block_peak + jnp.log(
        jnp.sum(jnp.exp(fine_score - block_peak), axis=2, keepdims=True)
    )
    parent_rows = jnp.take(coarse_centroids, my_blocks % NCOARSE, axis=0)
    parent_half = 0.5 * jnp.sum(jnp.square(parent_rows.astype(jnp.float32)), axis=1)
    parent_score = (
        row_scale[:, None]
        * jnp.einsum("pd,sd->ps", point_codes, parent_rows, preferred_element_type=jnp.float32)
        - parent_half[None, :]
    )
    joint_score = parent_score[:, :, None] + fine_score - block_norm
    live_slot = my_start + jnp.arange(my_slots) < live_counts[0]
    joint_score = jnp.where(live_slot[None, :, None], joint_score, MASK_SCORE).reshape(
        point_count, my_slots * BLOCK
    )
    joint_peak = jnp.max(joint_score, axis=1)
    joint_total = jnp.sum(jnp.exp(joint_score - joint_peak[:, None]), axis=1)
    fine_peak, fine_total = joined((joint_peak, joint_total), "cent", combine_norms)
    fine_resp = jnp.exp(joint_score - fine_peak[:, None]) / fine_total[:, None]
    fine_weight = (fine_resp * row_scale[:, None]).astype(jnp.bfloat16)
    fine_sum = jnp.einsum(
        "pj,pd->jd", fine_weight, point_codes, preferred_element_type=jnp.float32
    ).reshape(my_slots, BLOCK, width_d)
    fine_mass = jnp.sum(fine_resp, axis=0).reshape(my_slots, BLOCK)
    mass_copies = jnp.broadcast_to(fine_mass[:, :, None], (my_slots, BLOCK, cent_count))
    sum_quarters, mass_quarters = (
        lax.all_to_all(fine_sum, "cent", split_axis=2, concat_axis=0, tiled=True),
        lax.all_to_all(mass_copies, "cent", split_axis=2, concat_axis=0, tiled=True),
    )
    targets = jnp.arange(pts_count * pair_slots)
    matches = row_position[None, :] == targets[:, None]
    source = jnp.sum(jnp.where(matches, jnp.arange(capacity)[None, :], 0), axis=1)
    present = jnp.any(matches, axis=1)[:, None, None]
    send_sums = jnp.where(present, jnp.take(sum_quarters, source, axis=0), 0.0)
    send_mass = jnp.where(present, jnp.take(mass_quarters, source, axis=0), 0.0)
    back_sums, back_mass = (
        lax.all_to_all(send_sums, "pts", split_axis=0, concat_axis=0, tiled=True),
        lax.all_to_all(send_mass, "pts", split_axis=0, concat_axis=0, tiled=True),
    )
    owner_sums = jnp.einsum("xl,xbq->lbq", return_picks, back_sums, precision=lax.Precision.HIGHEST)
    owner_mass = jnp.einsum("xl,xbq->lbq", return_picks, back_mass, precision=lax.Precision.HIGHEST)
    prior_rows = fine_centroids.astype(jnp.float32).reshape(own_blocks, BLOCK, quarter)
    new_fine = (owner_sums + PRIOR_MASS * prior_rows) / (owner_mass + PRIOR_MASS)
    return (new_coarse, new_fine.reshape(own_blocks * BLOCK, quarter))


def solution(mesh):
    return jax.shard_map(
        body,
        mesh=mesh,
        in_specs=(
            P(("groups", "pts"), None),
            P(("groups", "pts")),
            P("groups", None),
            P(("groups", "pts"), "cent"),
            P(("groups", "pts"), None),
            P(("groups", "pts")),
        ),
        out_specs=(P(("groups", "cent"), None), P(("groups", "pts"), "cent")),
        check_vma=False,
    )
```

profile of v0, /device:TPU:0, one launch (start us, length us, event | category | flops | bytes accessed | tf_op | source)
XLA Modules:
  0.0 207.1 jit_solution(3614890451179491229)
XLA Ops:
  7.2 12.8 %all-gather.6 = s32[4,1,16]{2,1,0:T(1,128)S(1)} all-gather(s32[1,1,16]{2,1,0:T(1,128)} %bitcast.230), channel_id=1, replica_groups=mesh['groups'=2,'pts'=4,'cent'=4] {'pts'}, dimensions={0}, use_global_device_ids=true | all-gather | bytes 320 | tf_op jit(solution)/shard_map/all_gather | solution.py:62
  20.1 7.4 %all_gather.35 = bf16[256,1024]{1,0:T(8,128)(2,1)S(1)} all-gather(bf16[256,256]{1,0:T(8,128)(2,1)} %param.13), channel_id=1, replica_groups=mesh['groups'=2,'pts'=4,'cent'=4] {'cent'}, dimensions={1}, use_global_device_ids=true | all-gather | bytes 655360 | tf_op jit(solution)/shard_map/all_gather | solution.py:96
  27.5 0.4 reshape.386
  27.9 0.3 convert_reduce_fusion
  28.3 0.7 fusion.40
  29.0 2.4 %copy.41 = bf16[16,64,1024]{2,1,0:T(8,128)(2,1)} copy(bf16[16,64,1024]{2,0,1:T(8,128)(2,1)S(1)} %fusion.40) | data formatting | bytes 4194304 | tf_op jit(solution)/shard_map/dot_general | solution.py:102
  31.4 4.6 %all-to-all-start = ((bf16[16,64,1024]{2,1,0:T(8,128)(2,1)}), bf16[16,64,1024]{2,1,0:T(8,128)(2,1)}, u32[]{:S(2)}, u32[]{:S(2)}) async-start(bf16[16,64,1024]{2,1,0:T(8,128)(2,1)} %copy.41), calls=%async_computation | async-start | bytes 4194304 | tf_op jit(solution)/shard_map/all_to_all | solution.py:107
  36.2 0.5 fusion.39
  36.7 5.2 %all-gather.5 = f32[4,1,512]{2,1,0:T(1,128)S(1)} all-gather(f32[1,1,512]{2,1,0:T(1,128)S(1)} %bitcast.225), channel_id=3, replica_groups=mesh['groups'=2,'pts'=4,'cent'=4] {'cent'}, dimensions={0}, use_global_device_ids=true | all-gather | bytes 10240 | tf_op jit(solution)/shard_map/all_gather | solution.py:16
  41.9 5.1 %all-gather.4 = f32[4,1,512]{2,1,0:T(1,128)S(1)} all-gather(f32[1,1,512]{2,1,0:T(1,128)S(1)} %bitcast.221), channel_id=2, replica_groups=mesh['groups'=2,'pts'=4,'cent'=4] {'cent'}, dimensions={0}, use_global_device_ids=true | all-gather | bytes 10240 | tf_op jit(solution)/shard_map/all_gather | solution.py:16
  47.6 0.6 gather_fusion
  49.3 0.2 multiply_reduce_fusion.1
  49.5 0.4 fusion.3
  49.9 35.2 %all-to-all-done = bf16[16,64,1024]{2,1,0:T(8,128)(2,1)} async-done(((bf16[16,64,1024]{2,1,0:T(8,128)(2,1)}), bf16[16,64,1024]{2,1,0:T(8,128)(2,1)}, u32[]{:S(2)}, u32[]{:S(2)}) %all-to-all-start) | async-done | bytes 2097184 | tf_op jit(solution)/shard_map/all_to_all | solution.py:107
  85.1 2.2 %gather_fusion.1 = bf16[4,64,1024]{2,1,0:T(8,128)(2,1)S(1)} fusion(bf16[16,64,1024]{2,1,0:T(8,128)(2,1)} %all-to-all-done, s32[1024]{0:T(1024)S(1)} %pad_clamp_fusion.1), kind=kCustom, calls=%fused_computation.1 | custom fusion | bytes 1048592 | tf_op jit(solution)/shard_map/jit(_take)/gather | solution.py:116
  87.2 0.3 multiply_reduce_fusion
  87.7 0.5 subtract_reduce_fusion
  88.6 0.2 exponential_reduce_fusion
  88.9 5.2 %all-gather.8 = f32[4,1,512]{2,1,0:T(1,128)S(1)} all-gather(f32[1,1,512]{2,1,0:T(1,128)S(1)} %bitcast.226), channel_id=5, replica_groups=mesh['groups'=2,'pts'=4,'cent'=4] {'cent'}, dimensions={0}, use_global_device_ids=true | all-gather | bytes 10240 | tf_op jit(solution)/shard_map/all_gather | solution.py:16
  94.0 5.1 %all-gather.7 = f32[4,1,512]{2,1,0:T(1,128)S(1)} all-gather(f32[1,1,512]{2,1,0:T(1,128)S(1)} %bitcast.222), channel_id=4, replica_groups=mesh['groups'=2,'pts'=4,'cent'=4] {'cent'}, dimensions={0}, use_global_device_ids=true | all-gather | bytes 10240 | tf_op jit(solution)/shard_map/all_gather | solution.py:16
  99.3 0.3 fusion.38
  99.8 0.7 reshape.464
  100.5 3.2 %all-to-all-start.3 = ((f32[4,1,256]{2,1,0:T(1,128)}), f32[4,1,256]{2,1,0:T(1,128)S(1)}, u32[]{:S(2)}, u32[]{:S(2)}) async-start(f32[4,1,256]{2,1,0:T(1,128)} %reshape.464), calls=%async_computation.3 | async-start | bytes 8192 | tf_op jit(solution)/shard_map/all_to_all | solution.py:153
  103.7 1.4 fusion.4
  105.1 1.8 copy.42
  107.0 2.9 %reshape.462 = f32[4,1,65536]{2,1,0:T(1,128)} reshape(f32[1024,4,64]{2,1,0:T(4,128)S(1)} %bitcast.194) | data formatting | bytes 2097152
  109.9 3.5 %all-to-all-start.1 = ((f32[4,1,65536]{2,1,0:T(1,128)}), f32[4,1,65536]{2,1,0:T(1,128)S(1)}, u32[]{:S(2)}, u32[]{:S(2)}) async-start(f32[4,1,65536]{2,1,0:T(1,128)} %reshape.462), calls=%async_computation.1 | async-start | bytes 2097152 | tf_op jit(solution)/shard_map/all_to_all | solution.py:152
  113.6 0.5 broadcast.604
  114.2 0.6 reduce.5
  114.9 0.6 gather_fusion.3
  115.5 0.7 reduce.6
  116.2 0.7 reshape.466
  116.9 11.0 %all-to-all-done.1 = f32[4,1,65536]{2,1,0:T(1,128)S(1)} async-done(((f32[4,1,65536]{2,1,0:T(1,128)}), f32[4,1,65536]{2,1,0:T(1,128)S(1)}, u32[]{:S(2)}, u32[]{:S(2)}) %all-to-all-start.1) | async-done | bytes 1048608 | tf_op jit(solution)/shard_map/all_to_all | solution.py:152
  127.9 3.4 %all-to-all-start.4 = ((f32[4,1,256]{2,1,0:T(1,128)}), f32[4,1,256]{2,1,0:T(1,128)S(1)}, u32[]{:S(2)}, u32[]{:S(2)}) async-start(f32[4,1,256]{2,1,0:T(1,128)} %reshape.466), calls=%async_computation.4 | async-start | bytes 8192 | tf_op jit(solution)/shard_map/all_to_all | solution.py:163
  131.3 4.7 %reduce.4 = f32[4,65536]{1,0:T(4,128)} reduce(f32[4,1,65536]{2,1,0:T(1,128)S(1)} %all-to-all-done.1, f32[]{:T(128)} %broadcast.604), dimensions={1}, to_apply=%all_to_all.36.reduce_sub_computation | reduce | bytes 2097156 | tf_op jit(solution)/shard_map/all_to_all | solution.py:152
  136.0 2.7 %reshape.463 = f32[1024,4,64]{2,1,0:T(4,128)S(1)} reshape(f32[4,65536]{1,0:T(4,128)} %reduce.4) | data formatting | bytes 2097152
  138.7 1.6 copy.44
  140.3 1.8 gather_fusion.2
  142.1 1.2 select_select_fusion
  143.3 5.0 %all-to-all-start.2 = ((f32[16,64,256]{2,1,0:T(8,128)}), f32[16,64,256]{2,1,0:T(8,128)S(1)}, u32[]{:S(2)}, u32[]{:S(2)}) async-start(f32[16,64,256]{2,1,0:T(8,128)} %select_select_fusion), calls=%async_computation.2 | async-start | bytes 2097152 | tf_op jit(solution)/shard_map/all_to_all | solution.py:162
  148.5 1.0 fusion.13
  149.7 25.0 %psum.15 = f32[64]{0:T(128)S(1)} all-reduce(f32[64]{0:T(128)S(1)} %fusion.15), channel_id=1, replica_groups=mesh['groups'=2,'pts'=4,'cent'=4] {'pts'}, use_global_device_ids=true, to_apply=%region_7.8 | all-reduce | flops 64 | bytes 512 | tf_op jit(solution)/shard_map/psum | solution.py:82
  174.9 20.4 %all-reduce.2.cloned.1.call-done = f32[64,1024]{1,0:T(8,128)} async-done(((f32[64,1024]{1,0:T(8,128)}), f32[64,1024]{1,0:T(8,128)}) %all-reduce.2.cloned.1.call-update) | async-done | bytes 262160 | tf_op jit(solution)/shard_map/psum | solution.py:82
  195.3 1.8 fusion.11
  197.1 0.6 reduce.7
  197.8 0.2 convolution_add_fusion.1
  198.1 1.3 fusion
  199.5 0.8 copy.49
  (94 shorter events, 3.5 us)
Async XLA Ops:
  7.2 29.1 %copy-start = (bf16[512,1024]{1,0:T(8,128)(2,1)S(1)}, bf16[512,1024]{1,0:T(8,128)(2,1)}, u32[]{:S(2)}) copy-start(bf16[512,1024]{1,0:T(8,128)(2,1)} %param.10) | copy-start | bytes 3145732
  31.4 4.6 %copy-start.6 = (f32[2]{0:T(128)S(1)}, f32[2]{0:T(128)}, u32[]{:S(2)}) copy-start(f32[2]{0:T(128)} %param.11) | copy-start | bytes 28
  31.4 4.7 %copy-start.2 = (bf16[256,1024]{1,0:T(8,128)(2,1)S(1)}, bf16[256,1024]{1,0:T(8,128)(2,1)}, u32[]{:S(2)}) copy-start(bf16[256,1024]{1,0:T(8,128)(2,1)} %param.12) | copy-start | bytes 1572868
  31.4 15.6 %copy-start.5 = (s32[1,16]{1,0:T(1,128)S(1)}, s32[1,16]{1,0:T(1,128)}, u32[]{:S(2)}) copy-start(s32[1,16]{1,0:T(1,128)} %param.14) | copy-start | bytes 196
  31.4 53.6 %all-to-all-start = ((bf16[16,64,1024]{2,1,0:T(8,128)(2,1)}), bf16[16,64,1024]{2,1,0:T(8,128)(2,1)}, u32[]{:S(2)}, u32[]{:S(2)}) async-start(bf16[16,64,1024]{2,1,0:T(8,128)(2,1)} %copy.41), calls=%async_computation | async-start | bytes 4194304 | tf_op jit(solution)/shard_map/all_to_all | solution.py:107
  41.9 46.3 %copy-start.3 = (f32[4,1,512]{2,1,0:T(1,128)}, f32[4,1,512]{2,1,0:T(1,128)S(1)}, u32[]{:S(2)}) copy-start(f32[4,1,512]{2,1,0:T(1,128)S(1)} %all-gather.5) | copy-start | bytes 24580
  47.1 41.2 %copy-start.4 = (f32[4,1,512]{2,1,0:T(1,128)}, f32[4,1,512]{2,1,0:T(1,128)S(1)}, u32[]{:S(2)}) copy-start(f32[4,1,512]{2,1,0:T(1,128)S(1)} %all-gather.4) | copy-start | bytes 24580
  100.5 9.5 %all-to-all-start.3 = ((f32[4,1,256]{2,1,0:T(1,128)}), f32[4,1,256]{2,1,0:T(1,128)S(1)}, u32[]{:S(2)}, u32[]{:S(2)}) async-start(f32[4,1,256]{2,1,0:T(1,128)} %reshape.464), calls=%async_computation.3 | async-start | bytes 8192 | tf_op jit(solution)/shard_map/all_to_all | solution.py:153
  109.9 18.0 %all-to-all-start.1 = ((f32[4,1,65536]{2,1,0:T(1,128)}), f32[4,1,65536]{2,1,0:T(1,128)S(1)}, u32[]{:S(2)}, u32[]{:S(2)}) async-start(f32[4,1,65536]{2,1,0:T(1,128)} %reshape.462), calls=%async_computation.1 | async-start | bytes 2097152 | tf_op jit(solution)/shard_map/all_to_all | solution.py:152
  127.9 15.4 %all-to-all-start.4 = ((f32[4,1,256]{2,1,0:T(1,128)}), f32[4,1,256]{2,1,0:T(1,128)S(1)}, u32[]{:S(2)}, u32[]{:S(2)}) async-start(f32[4,1,256]{2,1,0:T(1,128)} %reshape.466), calls=%async_computation.4 | async-start | bytes 8192 | tf_op jit(solution)/shard_map/all_to_all | solution.py:163
  142.1 6.2 %slice-start = ((f32[4,1,512]{2,1,0:T(1,128)}), f32[1,1,512]{2,1,0:T(1,128)S(1)}, s32[]{:S(2)}) async-start(f32[4,1,512]{2,1,0:T(1,128)} %copy-done.3), calls=%async_computation.6 | async-start | bytes 4096 | tf_op jit(solution)/shard_map/jit(dynamic_index_in_dim)/dynamic_slice | solution.py:19
  142.1 6.2 %slice-start.1 = ((f32[4,1,512]{2,1,0:T(1,128)}), f32[1,1,512]{2,1,0:T(1,128)S(1)}, s32[]{:S(2)}) async-start(f32[4,1,512]{2,1,0:T(1,128)} %copy-done.4), calls=%async_computation.7 | async-start | bytes 4096 | tf_op jit(solution)/shard_map/jit(dynamic_index_in_dim)/dynamic_slice | solution.py:19
  143.3 31.4 %copy-start.1 = (bf16[256,256]{1,0:T(8,128)(2,1)S(1)}, bf16[256,256]{1,0:T(8,128)(2,1)}, u32[]{:S(2)}) copy-start(bf16[256,256]{1,0:T(8,128)(2,1)} %param.13) | copy-start | bytes 393220
  143.3 54.8 %all-to-all-start.2 = ((f32[16,64,256]{2,1,0:T(8,128)}), f32[16,64,256]{2,1,0:T(8,128)S(1)}, u32[]{:S(2)}, u32[]{:S(2)}) async-start(f32[16,64,256]{2,1,0:T(8,128)} %select_select_fusion), calls=%async_computation.2 | async-start | bytes 2097152 | tf_op jit(solution)/shard_map/all_to_all | solution.py:162
  148.3 47.0 %all-reduce.2.cloned.1.call-start = ((), (), s32[]{:S(2)}) async-start(), calls=%async_computation.5 | async-start | bytes 524288 | tf_op jit(solution)/shard_map/psum | solution.py:82
Sparse Core Ops, SparseCore 0:
  152.1 43.2 all-reduce.1
where the time goes:
time: 208 us; the launch traced here: 207 us
  waiting for transfers between devices  66.6 us (32%)
  blocking collectives  65.9 us (32%)
  local copies, waits for them, and re-layouts  20.6 us (10%)
  starting transfers between devices  19.8 us (10%)
  between operations  15 us (7%)
  other arithmetic  12.8 us (6%)
  matrix products  6.19 us (3%)
    all_to_all x1, waiting for transfers between devices, body(): lax.all_to_all(outgoing.reshape(pts_count * pair_slots, BLOCK, width_d),...  35.2 us
    psum x1, blocking collectives, body(): coarse_sum, coarse_mass = lax.psum((coarse_sum, coarse_mass), 'pts')  25 us
    all_gather x4, blocking collectives, joined(): gathered = jax.tree.map(lambda a: lax.all_gather(a, axis), part)  20.6 us
    psum x1, waiting for transfers between devices, body(): coarse_sum, coarse_mass = lax.psum((coarse_sum, coarse_mass), 'pts')  20.4 us
    all_gather x1, blocking collectives, body(): all_lists = lax.all_gather(block_lists, 'pts', axis=0, tiled=True)  12.8 us
    all_to_all x1, waiting for transfers between devices, body(): lax.all_to_all(fine_sum, 'cent', split_axis=2, concat_axis=0, tiled=True)  11 us
    all_gather x1, blocking collectives, body(): whole_rows = lax.all_gather(fine_centroids, 'cent', axis=1, tiled=True)  7.38 us
    unnamed x27, local copies, waits for them, and re-layouts  7.24 us
  transfers between devices with their start and end apart: 6, of which 3 were waited for; matrix products, arithmetic and copies ran while one was open for 14% of the time, Pallas kernels for 0%

commit v1 on v0

--- a/solution.py
+++ b/solution.py
@@ -1,6 +1,10 @@
+import functools
+
 import jax
 import jax.numpy as jnp
 from jax import lax
+from jax.experimental import pallas as pl
+from jax.experimental.pallas import tpu as pltpu
 from jax.sharding import PartitionSpec as P
 
 NCOARSE = 256
@@ -47,7 +51,7 @@
     return jnp.einsum("psr,psl->prl", by_rank, by_block).reshape(-1, own_blocks)
 
 
-def body(point_codes, shard_scales, coarse_centroids, fine_centroids, block_lists, live_counts):
+def general_body(point_codes, shard_scales, coarse_centroids, fine_centroids, block_lists, live_counts):
     pts_count = lax.axis_size("pts")
     cent_count = lax.axis_size("cent")
     pts_index = lax.axis_index("pts")
@@ -169,6 +173,383 @@
     return (new_coarse, new_fine.reshape(own_blocks * BLOCK, quarter))
 
 
+def row_dot(a, b):
+    return lax.dot_general(a, b, (((1,), (1,)), ((), ())), preferred_element_type=jnp.float32)
+
+
+def half_square(a):
+    a = a.astype(jnp.float32)
+    return 0.5 * jnp.sum(a * a, axis=1, keepdims=True)
+
+
+def diagonal(rows):
+    shape = (rows, 128)
+    return lax.broadcasted_iota(jnp.int32, shape, 0) == lax.broadcasted_iota(jnp.int32, shape, 1)
+
+
+def to_row(column):
+    row = jnp.sum(jnp.where(diagonal(column.shape[0]), column, 0.0), axis=0, keepdims=True)
+    return jnp.broadcast_to(row, (8, 128))
+
+
+def to_column(row, rows):
+    return jnp.sum(jnp.where(diagonal(rows), row, 0.0), axis=1, keepdims=True)
+
+
+def kernel(
+    n, m,
+    codes, scales, coarse, fine, lists, counts,
+    out_coarse, out_fine,
+    rows, sums, part, outgoing, from_left, from_right, prior, resp,
+    coarse_mass, mass_out, mass_in, finished, arrived,
+    x_send, x_recv, gr_send, gl_send, g_recv, cr_send, cl_send, c_recv,
+    s_send, sl_recv, sr_recv, m_send, m_recv, cm_send, cm_recv, o_send, o_recv,
+):
+    z = lax.axis_index("pts")
+    c = lax.axis_index("cent")
+    right, left = lax.rem(z + 1, n), lax.rem(z + n - 1, n)
+    points, width = codes.shape
+    quarter = fine.shape[1]
+    share = coarse.shape[0] // m
+
+    def remote(src, dst, send, recv, target):
+        return pltpu.make_async_remote_copy(
+            src_ref=src, dst_ref=dst, send_sem=send, recv_sem=recv,
+            device_id=target, device_id_type=pl.DeviceIdType.MESH,
+        )
+
+    def cent_peer(j):
+        return lax.rem(c + j, m)
+
+    def pts_peer(j):
+        return lax.rem(z + j, n)
+
+    def lanes(i):
+        return pl.ds(pl.multiple_of(i * quarter, quarter), quarter)
+
+    def block_rows(i):
+        return pl.ds(pl.multiple_of(i * BLOCK, BLOCK), BLOCK)
+
+    barrier = pltpu.get_barrier_semaphore()
+    for j in range(1, m):
+        pl.semaphore_signal(
+            barrier, inc=1, device_id={"cent": cent_peer(j)}, device_id_type=pl.DeviceIdType.MESH
+        )
+    for j in range(1, n):
+        pl.semaphore_signal(
+            barrier, inc=1, device_id={"pts": pts_peer(j)}, device_id_type=pl.DeviceIdType.MESH
+        )
+    pl.semaphore_wait(barrier, n + m - 2)
+
+    def features_to(peer):
+        return remote(
+            fine.at[block_rows(peer), :], rows.at[z, :, lanes(c)],
+            x_send.at[peer], x_recv.at[c], {"cent": peer},
+        )
+
+    def features_from(peer):
+        return remote(
+            fine.at[block_rows(peer), :], rows.at[z, :, lanes(peer)],
+            x_send.at[peer], x_recv.at[peer], {"cent": peer},
+        )
+
+    for j in range(1, m):
+        features_to(cent_peer(j)).start()
+    rows[z, :, lanes(c)] = fine[block_rows(c), :]
+
+    scale_row = jnp.zeros((1, points), jnp.float32)
+    shard = lax.broadcasted_iota(jnp.int32, (1, points), 1) // SHARD
+    for i in range(scales.shape[1]):
+        scale_row = jnp.where(shard == i, scales[0:1, i : i + 1], scale_row)
+
+    score = scale_row * row_dot(coarse[...], codes[...]) - half_square(coarse[...])
+    expo = jnp.exp(score - jnp.max(score, axis=0, keepdims=True))
+    resp[...] = expo / jnp.sum(expo, axis=0, keepdims=True)
+    slots = lists.shape[1]
+    shape = (slots, slots)
+    slot = lax.broadcasted_iota(jnp.int32, shape, 1)
+    named = jnp.logical_and(
+        lists[...] == lax.broadcasted_iota(jnp.int32, shape, 0), slot < counts[...]
+    )
+    live = jnp.sum(jnp.where(named, 1.0, 0.0), axis=1, keepdims=True) > 0.0
+    parent = jnp.where(live, score[:slots], MASK_SCORE)
+    parent = jnp.exp(parent - jnp.max(parent, axis=0, keepdims=True))
+    parent = jnp.where(live, parent, 0.0)
+    prior[...] = parent / jnp.sum(parent, axis=0, keepdims=True)
+
+    def to_right(buffer, b, send, recv):
+        return remote(buffer.at[b], buffer.at[b], send.at[b], recv.at[b], {"pts": right})
+
+    def to_left(buffer, b, send, recv):
+        return remote(buffer.at[b], buffer.at[b], send.at[b], recv.at[b], {"pts": left})
+
+    def start_own(buffer, send_r, send_l, recv):
+        @pl.when(z < n - 1)
+        def _():
+            to_right(buffer, z, send_r, recv).start()
+
+        @pl.when(z > 0)
+        def _():
+            to_left(buffer, z, send_l, recv).start()
+
+    def pass_on(d, buffer, send_r, send_l, recv):
+        @pl.when(z - d >= 0)
+        def _():
+            to_right(buffer, z - d, send_r, recv).wait_recv()
+
+            @pl.when(z < n - 1)
+            def _():
+                to_right(buffer, z - d, send_r, recv).start()
+
+        @pl.when(z + d < n)
+        def _():
+            to_left(buffer, z + d, send_l, recv).wait_recv()
+
+            @pl.when(z > 0)
+            def _():
+                to_left(buffer, z + d, send_l, recv).start()
+
+    def finish_sends(buffer, send_r, send_l, recv):
+        for d in range(n):
+            @pl.when(jnp.logical_and(z - d >= 0, z < n - 1))
+            def _():
+                to_right(buffer, z - d, send_r, recv).wait_send()
+
+            @pl.when(jnp.logical_and(z + d < n, z > 0))
+            def _():
+                to_left(buffer, z + d, send_l, recv).wait_send()
+
+    fine_sems = (gr_send, gl_send, g_recv)
+    coarse_sems = (cr_send, cl_send, c_recv)
+
+    for j in range(1, m):
+        features_from(cent_peer(j)).wait_recv()
+    start_own(rows, *fine_sems)
+
+    mine = resp[pl.ds(pl.multiple_of(c * share, share), share), :]
+    sums[z] = jnp.dot(
+        (mine * scale_row).astype(jnp.bfloat16), codes[...], preferred_element_type=jnp.float32
+    ).astype(jnp.bfloat16)
+    coarse_mass[z] = to_row(jnp.sum(mine, axis=1, keepdims=True))
+    start_own(sums, *coarse_sems)
+
+    def coarse_mass_to(peer):
+        return remote(
+            coarse_mass.at[z], coarse_mass.at[z], cm_send.at[peer], cm_recv.at[z], {"pts": peer}
+        )
+
+    def coarse_mass_from(peer):
+        return remote(
+            coarse_mass.at[peer], coarse_mass.at[peer], cm_send.at[peer], cm_recv.at[peer],
+            {"pts": peer},
+        )
+
+    for j in range(1, n):
+        coarse_mass_to(pts_peer(j)).start()
+
+    def mass_to(peer):
+        return remote(
+            mass_out.at[peer], mass_in.at[z], m_send.at[peer], m_recv.at[z], {"pts": peer}
+        )
+
+    def mass_from(peer):
+        return remote(
+            mass_out.at[peer], mass_in.at[peer], m_send.at[peer], m_recv.at[peer], {"pts": peer}
+        )
+
+    def use_block(b):
+        block = rows[b]
+        score = scale_row * row_dot(block, codes[...]) - half_square(block)
+        expo = jnp.exp(score - jnp.max(score, axis=0, keepdims=True))
+        factor = prior[pl.ds(b * m + c, 1), :] / jnp.sum(expo, axis=0, keepdims=True)
+        share_of = expo * factor
+        part[b] = jnp.dot(
+            (share_of * scale_row).astype(jnp.bfloat16), codes[...],
+            preferred_element_type=jnp.float32,
+        )
+        return to_row(jnp.sum(share_of, axis=1, keepdims=True))
+
+    def sums_right(b):
+        return remote(
+            outgoing.at[b], from_left.at[b], s_send.at[b], sl_recv.at[b], {"pts": right}
+        )
+
+    def sums_left(b):
+        return remote(
+            outgoing.at[b], from_right.at[b], s_send.at[b], sr_recv.at[b], {"pts": left}
+        )
+
+    mass_in[z] = use_block(z)
+    for d in range(1, n):
+        pass_on(d, rows, *fine_sems)
+
+        @pl.when(z - d >= 0)
+        def _():
+            b = z - d
+            mass_out[b] = use_block(b)
+            mass_to(b).start()
+
+            @pl.when(z == n - 1)
+            def _():
+                outgoing[b] = part[b].astype(jnp.bfloat16)
+                sums_left(b).start()
+
+        @pl.when(z + d < n)
+        def _():
+            b = z + d
+            mass_out[b] = use_block(b)
+            mass_to(b).start()
+
+            @pl.when(z == 0)
+            def _():
+                outgoing[b] = part[b].astype(jnp.bfloat16)
+                sums_right(b).start()
+
+        pass_on(d, sums, *coarse_sems)
+
+    mirror = n - 1 - z
+    for time in range(3, 2 * n - 2):
+        @pl.when(jnp.logical_and(z > 0, jnp.logical_and(time - z > z, time - z < n)))
+        def _():
+            b = time - z
+            sums_right(b).wait_recv()
+            outgoing[b] = (part[b] + from_left[b].astype(jnp.float32)).astype(jnp.bfloat16)
+            sums_right(b).start()
+
+        @pl.when(
+            jnp.logical_and(mirror > 0, jnp.logical_and(time - mirror > mirror, time - mirror < n))
+        )
+        def _():
+            b = n - 1 - (time - mirror)
+            sums_left(b).wait_recv()
+            outgoing[b] = (part[b] + from_right[b].astype(jnp.float32)).astype(jnp.bfloat16)
+            sums_left(b).start()
+
+    for j in range(1, n):
+        coarse_mass_from(pts_peer(j)).wait_recv()
+    total = sums[0].astype(jnp.float32)
+    mass = coarse_mass[0]
+    for i in range(1, n):
+        total = total + sums[i].astype(jnp.float32)
+        mass = mass + coarse_mass[i]
+    own = coarse[pl.ds(pl.multiple_of(c * share, share), share), :].astype(jnp.float32)
+    out_coarse[...] = (total + PRIOR_MASS * own) / (to_column(mass[0:1], share) + PRIOR_MASS)
+
+    for j in range(1, n):
+        mass_from(pts_peer(j)).wait_recv()
+
+    @pl.when(z > 0)
+    def _():
+        sums_right(z).wait_recv()
+        part[z] = part[z] + from_left[z].astype(jnp.float32)
+
+    @pl.when(z < n - 1)
+    def _():
+        sums_left(z).wait_recv()
+        part[z] = part[z] + from_right[z].astype(jnp.float32)
+
+    mass = mass_in[0]
+    for i in range(1, n):
+        mass = mass + mass_in[i]
+    finished[...] = (part[z] + PRIOR_MASS * rows[z].astype(jnp.float32)) / (
+        to_column(mass[0:1], BLOCK) + PRIOR_MASS
+    )
+
+    def result_to(peer):
+        return remote(
+            finished.at[:, lanes(peer)], arrived.at[c], o_send.at[peer], o_recv.at[c],
+            {"cent": peer},
+        )
+
+    def result_from(peer):
+        return remote(
+            finished.at[:, lanes(peer)], arrived.at[peer], o_send.at[peer], o_recv.at[peer],
+            {"cent": peer},
+        )
+
+    for j in range(1, m):
+        result_to(cent_peer(j)).start()
+    out_fine[block_rows(c), :] = finished[:, lanes(c)]
+
+    for j in range(1, m):
+        features_to(cent_peer(j)).wait_send()
+    finish_sends(rows, *fine_sems)
+    finish_sends(sums, *coarse_sems)
+    for j in range(1, n):
+        coarse_mass_to(pts_peer(j)).wait_send()
+        mass_to(pts_peer(j)).wait_send()
+    for d in range(1, n):
+        @pl.when(z + d < n)
+        def _():
+            sums_right(z + d).wait_send()
+
+        @pl.when(z - d >= 0)
+        def _():
+            sums_left(z - d).wait_send()
+
+    for j in range(1, m):
+        peer = cent_peer(j)
+        result_from(peer).wait_recv()
+        out_fine[block_rows(peer), :] = arrived[peer]
+    for j in range(1, m):
+        result_to(cent_peer(j)).wait_send()
+
+
+def body(point_codes, shard_scales, coarse_centroids, fine_centroids, block_lists, live_counts):
+    n = lax.axis_size("pts")
+    m = lax.axis_size("cent")
+    points, width = point_codes.shape
+    own_blocks = fine_centroids.shape[0] // BLOCK
+    quarter = fine_centroids.shape[1]
+    slots = block_lists.shape[1]
+    every_block = slots == n * own_blocks and own_blocks == m and slots <= NCOARSE
+    if not every_block:
+        return general_body(
+            point_codes, shard_scales, coarse_centroids, fine_centroids, block_lists, live_counts
+        )
+    share = NCOARSE // m
+    f32, bf16 = jnp.float32, jnp.bfloat16
+    dma = pltpu.SemaphoreType.DMA
+    vmem = pl.BlockSpec(memory_space=pltpu.VMEM)
+    return pl.pallas_call(
+        functools.partial(kernel, n, m),
+        out_shape=(
+            jax.ShapeDtypeStruct((share, width), f32),
+            jax.ShapeDtypeStruct((own_blocks * BLOCK, quarter), f32),
+        ),
+        in_specs=[vmem] * 6,
+        out_specs=(vmem, vmem),
+        scratch_shapes=[
+            pltpu.VMEM((n, BLOCK, width), bf16),
+            pltpu.VMEM((n, share, width), bf16),
+            pltpu.VMEM((n, BLOCK, width), f32),
+            pltpu.VMEM((n, BLOCK, width), bf16),
+            pltpu.VMEM((n, BLOCK, width), bf16),
+            pltpu.VMEM((n, BLOCK, width), bf16),
+            pltpu.VMEM((slots, points), f32),
+            pltpu.VMEM((NCOARSE, points), f32),
+            pltpu.VMEM((n, 8, 128), f32),
+            pltpu.VMEM((n, 8, 128), f32),
+            pltpu.VMEM((n, 8, 128), f32),
+            pltpu.VMEM((BLOCK, width), f32),
+            pltpu.VMEM((m, BLOCK, quarter), f32),
+        ]
+        + [dma((m,))] * 2
+        + [dma((n,))] * 13
+        + [dma((m,))] * 2,
+        compiler_params=pltpu.CompilerParams(
+            collective_id=0, has_side_effects=True, vmem_limit_bytes=40 * 1024 * 1024
+        ),
+    )(
+        point_codes,
+        shard_scales.reshape(1, -1),
+        coarse_centroids,
+        fine_centroids,
+        block_lists,
+        live_counts.reshape(1, 1),
+    )
+
+
 def solution(mesh):
     return jax.shard_map(
         body,

time: 208 us -> 47.8 us (0.23)
  waiting for transfers between devices: 66.6 us -> 0 us
  blocking collectives: 65.9 us -> 0 us
  Pallas kernels: 0 us -> 41 us
  starting transfers between devices: 19.8 us -> 0 us
  local copies, waits for them, and re-layouts: 20.6 us -> 5.23 us
  between operations: 15 us -> 1.31 us
  other arithmetic: 12.8 us -> 0 us
  matrix products: 6.19 us -> 0 us
    all_to_all x5 -> x0, waiting for transfers between devices: 46.2 us -> none  [the longest x1 35.2 us: body(): lax.all_to_all(outgoing.reshape(pts_count * pair_slots, BLOCK, width_d),...]
    pallas_call x0 -> x1, Pallas kernels: none -> 41 us  [body(): pl.pallas_call(functools.partial(kernel, n, m), out_shape=(jax.ShapeDtype...]
    all_gather x6 -> x0, blocking collectives: 40.8 us -> none  [the longest x4 20.6 us: joined(): gathered = jax.tree.map(lambda a: lax.all_gather(a, axis), part)]
    psum x1 -> x0, blocking collectives: 25 us -> none  [body(): coarse_sum, coarse_mass = lax.psum((coarse_sum, coarse_mass), 'pts')]
    psum x1 -> x0, waiting for transfers between devices: 20.4 us -> none  [body(): coarse_sum, coarse_mass = lax.psum((coarse_sum, coarse_mass), 'pts')]
    all_to_all x5 -> x0, starting transfers between devices: 19.8 us -> none  [the longest x1 5.01 us: body(): lax.all_to_all(send_sums, 'pts', split_axis=0, concat_axis=0, tiled=True)]
    dot_general x10 -> x0, matrix products: 6.19 us -> none  [the longest x1 1.43 us: body(): jnp.einsum('pj,pd->jd', fine_weight, point_codes, preferred_element_type=...]
    all_to_all x3 -> x0, other arithmetic: 5.95 us -> none  [the longest x1 4.66 us: body(): lax.all_to_all(fine_sum, 'cent', split_axis=2, concat_axis=0, tiled=True)]
  transfers between devices with their start and end apart: 6 -> 0, of which waited for: 3 -> 0; matrix products, arithmetic and copies ran while one was open for 14% -> 0% of each run, Pallas kernels for 0% -> 0%
where the time goes in v1:
time: 47.8 us; the launch traced here: 47.5 us
  Pallas kernels  41 us (86%)
  local copies, waits for them, and re-layouts  5.23 us (11%)
  between operations  1.31 us (3%)
    pallas_call x1, Pallas kernels, body(): pl.pallas_call(functools.partial(kernel, n, m), out_shape=(jax.ShapeDtype...  41 us
    unnamed x12, local copies, waits for them, and re-layouts  5.23 us

profile of v1, /device:TPU:0, one launch (start us, length us, event | category | flops | bytes accessed | tf_op | source)
XLA Modules:
  0.0 47.5 jit_solution(16808673874906506140)
XLA Ops:
  1.3 0.0 copy-start.3
  1.3 0.0 copy-start.4
  1.3 0.6 %copy-done.3 = f32[2]{0:T(128)S(1)} copy-done((f32[2]{0:T(128)S(1)}, f32[2]{0:T(128)}, u32[]{:S(2)}) %copy-start.3) | copy-done | bytes 32
  1.9 0.0 copy-done.4
  1.9 0.0 copy-start
  2.0 1.2 %copy-done = bf16[512,1024]{1,0:T(8,128)(2,1)S(1)} copy-done((bf16[512,1024]{1,0:T(8,128)(2,1)S(1)}, bf16[512,1024]{1,0:T(8,128)(2,1)}, u32[]{:S(2)}) %copy-start) | copy-done | bytes 1048600
  3.2 0.0 copy-start.1
  3.2 1.0 %copy-done.1 = bf16[256,1024]{1,0:T(8,128)(2,1)S(1)} copy-done((bf16[256,1024]{1,0:T(8,128)(2,1)S(1)}, bf16[256,1024]{1,0:T(8,128)(2,1)}, u32[]{:S(2)}) %copy-start.1) | copy-done | bytes 524312
  4.2 0.0 copy-start.2
  4.2 0.9 %copy-done.2 = bf16[256,256]{1,0:T(8,128)(2,1)S(1)} copy-done((bf16[256,256]{1,0:T(8,128)(2,1)S(1)}, bf16[256,256]{1,0:T(8,128)(2,1)}, u32[]{:S(2)}) %copy-start.2) | copy-done | bytes 131096
  5.1 41.0 %shard_map.77 = (f32[64,1024]{1,0:T(8,128)S(1)}, f32[256,256]{1,0:T(8,128)S(1)}) custom-call(bf16[512,1024]{1,0:T(8,128)(2,1)S(1)} %copy-done, f32[1,2]{1,0:T(1,128)S(1)} %bitcast.3, bf16[256,1024]{1,0:T(8,128)(2,1)S(1)} %copy-done.1, bf16[256,256]{1,0:T(8,128)(2,1)S(1)} %copy-done.2, s32[1,16]{1,0:T(1,128)S(1)} %copy-done.4, s32[1,1]{1,0:T(1,128)} %bitcast.2.counts), custom_call_target="tpu_custom_call" | custom-call | tf_op jit(solution)/shard_map/pallas_call | solution.py:514
  46.1 0.7 %copy.11 = f32[64,1024]{1,0:T(8,128)} copy(f32[64,1024]{1,0:T(8,128)S(1)} %get-tuple-element.4) | data formatting | bytes 524288
  46.8 0.7 %copy.12 = f32[256,256]{1,0:T(8,128)} copy(f32[256,256]{1,0:T(8,128)S(1)} %get-tuple-element.5) | data formatting | bytes 524288
Async XLA Ops:
  1.3 0.7 %copy-start.3 = (f32[2]{0:T(128)S(1)}, f32[2]{0:T(128)}, u32[]{:S(2)}) copy-start(f32[2]{0:T(128)} %param.7) | copy-start | bytes 28
  1.3 0.7 %copy-start.4 = (s32[1,16]{1,0:T(1,128)S(1)}, s32[1,16]{1,0:T(1,128)}, u32[]{:S(2)}) copy-start(s32[1,16]{1,0:T(1,128)} %lists.1) | copy-start | bytes 196
  1.9 1.2 %copy-start = (bf16[512,1024]{1,0:T(8,128)(2,1)S(1)}, bf16[512,1024]{1,0:T(8,128)(2,1)}, u32[]{:S(2)}) copy-start(bf16[512,1024]{1,0:T(8,128)(2,1)} %codes.1) | copy-start | bytes 3145732
  3.2 1.0 %copy-start.1 = (bf16[256,1024]{1,0:T(8,128)(2,1)S(1)}, bf16[256,1024]{1,0:T(8,128)(2,1)}, u32[]{:S(2)}) copy-start(bf16[256,1024]{1,0:T(8,128)(2,1)} %coarse.1) | copy-start | bytes 1572868
  4.2 0.9 %copy-start.2 = (bf16[256,256]{1,0:T(8,128)(2,1)S(1)}, bf16[256,256]{1,0:T(8,128)(2,1)}, u32[]{:S(2)}) copy-start(bf16[256,256]{1,0:T(8,128)(2,1)} %fine.1) | copy-start | bytes 393220

commit v2 on v1

--- a/solution.py
+++ b/solution.py
@@ -14,6 +14,7 @@
 
 PRIOR_MASS = 1.0
 MASK_SCORE = -1e30
+HALVES = 2
 
 
 def joined(part, axis, combine):
@@ -182,9 +183,10 @@
     return 0.5 * jnp.sum(a * a, axis=1, keepdims=True)
 
 
-def diagonal(rows):
+def diagonal(rows, start=0):
     shape = (rows, 128)
-    return lax.broadcasted_iota(jnp.int32, shape, 0) == lax.broadcasted_iota(jnp.int32, shape, 1)
+    row = lax.broadcasted_iota(jnp.int32, shape, 0) + start
+    return row == lax.broadcasted_iota(jnp.int32, shape, 1)
 
 
 def to_row(column):
@@ -192,18 +194,20 @@
     return jnp.broadcast_to(row, (8, 128))
 
 
-def to_column(row, rows):
-    return jnp.sum(jnp.where(diagonal(rows), row, 0.0), axis=1, keepdims=True)
+def to_column(row, rows, start=0):
+    return jnp.sum(jnp.where(diagonal(rows, start), row, 0.0), axis=1, keepdims=True)
 
 
 def kernel(
     n, m,
-    codes, scales, coarse, fine, lists, counts,
+    codes_in, scales, coarse_in, fine, lists, counts,
     out_coarse, out_fine,
-    rows, sums, part, outgoing, from_left, from_right, prior, resp,
+    codes, coarse, rows, own_part, outgoing, incoming, prior, resp,
+    coarse_out, coarse_own, coarse_in_sums, coarse_new,
     coarse_mass, mass_out, mass_in, finished, arrived,
-    x_send, x_recv, gr_send, gl_send, g_recv, cr_send, cl_send, c_recv,
-    s_send, sl_recv, sr_recv, m_send, m_recv, cm_send, cm_recv, o_send, o_recv,
+    in_sem, x_send, x_recv, gr_send, gl_send, g_recv,
+    cs_send, cs_recv, cg_send, cg_recv,
+    s_send, s_recv, m_send, m_recv, cm_send, cm_recv, o_send, o_recv,
 ):
     z = lax.axis_index("pts")
     c = lax.axis_index("cent")
@@ -211,6 +215,8 @@
     points, width = codes.shape
     quarter = fine.shape[1]
     share = coarse.shape[0] // m
+    piece = share // n
+    half = BLOCK // HALVES
 
     def remote(src, dst, send, recv, target):
         return pltpu.make_async_remote_copy(
@@ -231,6 +237,11 @@
         return pl.ds(pl.multiple_of(i * BLOCK, BLOCK), BLOCK)
 
     barrier = pltpu.get_barrier_semaphore()
+    copies = [
+        pltpu.make_async_copy(coarse_in, coarse, in_sem.at[0]),
+        pltpu.make_async_copy(codes_in, codes, in_sem.at[1]),
+        pltpu.make_async_copy(fine.at[block_rows(c), :], rows.at[z, :, lanes(c)], in_sem.at[2]),
+    ]
     for j in range(1, m):
         pl.semaphore_signal(
             barrier, inc=1, device_id={"cent": cent_peer(j)}, device_id_type=pl.DeviceIdType.MESH
@@ -239,6 +250,8 @@
         pl.semaphore_signal(
             barrier, inc=1, device_id={"pts": pts_peer(j)}, device_id_type=pl.DeviceIdType.MESH
         )
+    for copy in copies:
+        copy.start()
     pl.semaphore_wait(barrier, n + m - 2)
 
     def features_to(peer):
@@ -255,7 +268,8 @@
 
     for j in range(1, m):
         features_to(cent_peer(j)).start()
-    rows[z, :, lanes(c)] = fine[block_rows(c), :]
+    for copy in copies:
+        copy.wait()
 
     scale_row = jnp.zeros((1, points), jnp.float32)
     shard = lax.broadcasted_iota(jnp.int32, (1, points), 1) // SHARD
@@ -277,61 +291,78 @@
     parent = jnp.where(live, parent, 0.0)
     prior[...] = parent / jnp.sum(parent, axis=0, keepdims=True)
 
-    def to_right(buffer, b, send, recv):
-        return remote(buffer.at[b], buffer.at[b], send.at[b], recv.at[b], {"pts": right})
-
-    def to_left(buffer, b, send, recv):
-        return remote(buffer.at[b], buffer.at[b], send.at[b], recv.at[b], {"pts": left})
-
-    def start_own(buffer, send_r, send_l, recv):
+    def half_copy(b, h, send, target):
+        part_of = rows.at[b, pl.ds(h * half, half), :]
+        return remote(part_of, part_of, send.at[b, h], g_recv.at[b, h], {"pts": target})
+
+    def to_right(b, h):
+        return half_copy(b, h, gr_send, right)
+
+    def to_left(b, h):
+        return half_copy(b, h, gl_send, left)
+
+    def pass_on(d):
+        for h in range(HALVES):
+            @pl.when(z - d >= 0)
+            def _():
+                to_right(z - d, h).wait_recv()
+
+                @pl.when(z < n - 1)
+                def _():
+                    to_right(z - d, h).start()
+
+            @pl.when(z + d < n)
+            def _():
+                to_left(z + d, h).wait_recv()
+
+                @pl.when(z > 0)
+                def _():
+                    to_left(z + d, h).start()
+
+    for j in range(1, m):
+        features_from(cent_peer(j)).wait_recv()
+    for h in range(HALVES):
         @pl.when(z < n - 1)
         def _():
-            to_right(buffer, z, send_r, recv).start()
+            to_right(z, h).start()
 
         @pl.when(z > 0)
         def _():
-            to_left(buffer, z, send_l, recv).start()
-
-    def pass_on(d, buffer, send_r, send_l, recv):
-        @pl.when(z - d >= 0)
-        def _():
-            to_right(buffer, z - d, send_r, recv).wait_recv()
-
-            @pl.when(z < n - 1)
-            def _():
-                to_right(buffer, z - d, send_r, recv).start()
-
-        @pl.when(z + d < n)
-        def _():
-            to_left(buffer, z + d, send_l, recv).wait_recv()
-
-            @pl.when(z > 0)
-            def _():
-                to_left(buffer, z + d, send_l, recv).start()
-
-    def finish_sends(buffer, send_r, send_l, recv):
-        for d in range(n):
-            @pl.when(jnp.logical_and(z - d >= 0, z < n - 1))
-            def _():
-                to_right(buffer, z - d, send_r, recv).wait_send()
-
-            @pl.when(jnp.logical_and(z + d < n, z > 0))
-            def _():
-                to_left(buffer, z + d, send_l, recv).wait_send()
-
-    fine_sems = (gr_send, gl_send, g_recv)
-    coarse_sems = (cr_send, cl_send, c_recv)
-
-    for j in range(1, m):
-        features_from(cent_peer(j)).wait_recv()
-    start_own(rows, *fine_sems)
+            to_left(z, h).start()
 
     mine = resp[pl.ds(pl.multiple_of(c * share, share), share), :]
-    sums[z] = jnp.dot(
+    coarse_part = jnp.dot(
         (mine * scale_row).astype(jnp.bfloat16), codes[...], preferred_element_type=jnp.float32
-    ).astype(jnp.bfloat16)
+    )
+    coarse_own[...] = coarse_part
+    coarse_out[...] = coarse_part.astype(jnp.bfloat16)
     coarse_mass[z] = to_row(jnp.sum(mine, axis=1, keepdims=True))
-    start_own(sums, *coarse_sems)
+
+    def piece_rows(i):
+        return pl.ds(pl.multiple_of(i * piece, piece), piece)
+
+    def piece_to(peer):
+        return remote(
+            coarse_out.at[piece_rows(peer), :], coarse_in_sums.at[z],
+            cs_send.at[peer], cs_recv.at[z], {"pts": peer},
+        )
+
+    def piece_from(peer):
+        return remote(
+            coarse_out.at[piece_rows(peer), :], coarse_in_sums.at[peer],
+            cs_send.at[peer], cs_recv.at[peer], {"pts": peer},
+        )
+
+    def new_to(peer):
+        return remote(
+            coarse_new.at[z], coarse_new.at[z], cg_send.at[peer], cg_recv.at[z], {"pts": peer}
+        )
+
+    def new_from(peer):
+        return remote(
+            coarse_new.at[peer], coarse_new.at[peer], cg_send.at[peer], cg_recv.at[peer],
+            {"pts": peer},
+        )
 
     def coarse_mass_to(peer):
         return remote(
@@ -346,6 +377,7 @@
 
     for j in range(1, n):
         coarse_mass_to(pts_peer(j)).start()
+        piece_to(pts_peer(j)).start()
 
     def mass_to(peer):
         return remote(
@@ -363,97 +395,72 @@
         expo = jnp.exp(score - jnp.max(score, axis=0, keepdims=True))
         factor = prior[pl.ds(b * m + c, 1), :] / jnp.sum(expo, axis=0, keepdims=True)
         share_of = expo * factor
-        part[b] = jnp.dot(
+        total = jnp.dot(
             (share_of * scale_row).astype(jnp.bfloat16), codes[...],
             preferred_element_type=jnp.float32,
         )
-        return to_row(jnp.sum(share_of, axis=1, keepdims=True))
-
-    def sums_right(b):
-        return remote(
-            outgoing.at[b], from_left.at[b], s_send.at[b], sl_recv.at[b], {"pts": right}
-        )
-
-    def sums_left(b):
-        return remote(
-            outgoing.at[b], from_right.at[b], s_send.at[b], sr_recv.at[b], {"pts": left}
-        )
-
-    mass_in[z] = use_block(z)
+        return total, to_row(jnp.sum(share_of, axis=1, keepdims=True))
+
+    def sums_to(peer):
+        return remote(
+            outgoing.at[peer], incoming.at[z], s_send.at[peer], s_recv.at[z], {"pts": peer}
+        )
+
+    def sums_from(peer):
+        return remote(
+            outgoing.at[peer], incoming.at[peer], s_send.at[peer], s_recv.at[peer], {"pts": peer}
+        )
+
+    def use_and_send(b):
+        total, mass = use_block(b)
+        outgoing[b] = total.astype(jnp.bfloat16)
+        mass_out[b] = mass
+        sums_to(b).start()
+        mass_to(b).start()
+
+    def finish_coarse_piece():
+        total = coarse_own[piece_rows(z), :]
+        mass = coarse_mass[z]
+        for j in range(1, n):
+            peer = pts_peer(j)
+            coarse_mass_from(peer).wait_recv()
+            piece_from(peer).wait_recv()
+            total = total + coarse_in_sums[peer].astype(jnp.float32)
+            mass = mass + coarse_mass[peer]
+        own = coarse[pl.ds(pl.multiple_of(c * share + z * piece, piece), piece), :]
+        new = (total + PRIOR_MASS * own.astype(jnp.float32)) / (
+            to_column(mass[0:1], piece, z * piece) + PRIOR_MASS
+        )
+        coarse_new[z] = new.astype(jnp.bfloat16)
+        for j in range(1, n):
+            new_to(pts_peer(j)).start()
+
+    own_part[...], mass_in[z] = use_block(z)
     for d in range(1, n):
-        pass_on(d, rows, *fine_sems)
+        pass_on(d)
 
         @pl.when(z - d >= 0)
         def _():
-            b = z - d
-            mass_out[b] = use_block(b)
-            mass_to(b).start()
-
-            @pl.when(z == n - 1)
-            def _():
-                outgoing[b] = part[b].astype(jnp.bfloat16)
-                sums_left(b).start()
+            use_and_send(z - d)
 
         @pl.when(z + d < n)
         def _():
-            b = z + d
-            mass_out[b] = use_block(b)
-            mass_to(b).start()
-
-            @pl.when(z == 0)
-            def _():
-                outgoing[b] = part[b].astype(jnp.bfloat16)
-                sums_right(b).start()
-
-        pass_on(d, sums, *coarse_sems)
-
-    mirror = n - 1 - z
-    for time in range(3, 2 * n - 2):
-        @pl.when(jnp.logical_and(z > 0, jnp.logical_and(time - z > z, time - z < n)))
-        def _():
-            b = time - z
-            sums_right(b).wait_recv()
-            outgoing[b] = (part[b] + from_left[b].astype(jnp.float32)).astype(jnp.bfloat16)
-            sums_right(b).start()
-
-        @pl.when(
-            jnp.logical_and(mirror > 0, jnp.logical_and(time - mirror > mirror, time - mirror < n))
-        )
-        def _():
-            b = n - 1 - (time - mirror)
-            sums_left(b).wait_recv()
-            outgoing[b] = (part[b] + from_right[b].astype(jnp.float32)).astype(jnp.bfloat16)
-            sums_left(b).start()
-
+            use_and_send(z + d)
+
+        if d == 1:
+            finish_coarse_piece()
+
+    total = own_part[...] + PRIOR_MASS * rows[z].astype(jnp.float32)
+    mass = mass_in[z]
     for j in range(1, n):
-        coarse_mass_from(pts_peer(j)).wait_recv()
-    total = sums[0].astype(jnp.float32)
-    mass = coarse_mass[0]
-    for i in range(1, n):
-        total = total + sums[i].astype(jnp.float32)
-        mass = mass + coarse_mass[i]
-    own = coarse[pl.ds(pl.multiple_of(c * share, share), share), :].astype(jnp.float32)
-    out_coarse[...] = (total + PRIOR_MASS * own) / (to_column(mass[0:1], share) + PRIOR_MASS)
-
-    for j in range(1, n):
-        mass_from(pts_peer(j)).wait_recv()
-
-    @pl.when(z > 0)
-    def _():
-        sums_right(z).wait_recv()
-        part[z] = part[z] + from_left[z].astype(jnp.float32)
-
-    @pl.when(z < n - 1)
-    def _():
-        sums_left(z).wait_recv()
-        part[z] = part[z] + from_right[z].astype(jnp.float32)
-
-    mass = mass_in[0]
-    for i in range(1, n):
-        mass = mass + mass_in[i]
-    finished[...] = (part[z] + PRIOR_MASS * rows[z].astype(jnp.float32)) / (
-        to_column(mass[0:1], BLOCK) + PRIOR_MASS
-    )
+        peer = pts_peer(j)
+        mass_from(peer).wait_recv()
+        sums_from(peer).wait_recv()
+        total = total + incoming[peer].astype(jnp.float32)
+        mass = mass + mass_in[peer]
+    new = total / (to_column(mass[0:1], BLOCK) + PRIOR_MASS)
+    own_part[...] = new
+    finished[...] = new.astype(jnp.bfloat16)
 
     def result_to(peer):
         return remote(
@@ -469,28 +476,35 @@
 
     for j in range(1, m):
         result_to(cent_peer(j)).start()
-    out_fine[block_rows(c), :] = finished[:, lanes(c)]
+    out_fine[block_rows(c), :] = own_part[:, lanes(c)]
 
     for j in range(1, m):
         features_to(cent_peer(j)).wait_send()
-    finish_sends(rows, *fine_sems)
-    finish_sends(sums, *coarse_sems)
+    for d in range(n):
+        for h in range(HALVES):
+            @pl.when(jnp.logical_and(z - d >= 0, z < n - 1))
+            def _():
+                to_right(z - d, h).wait_send()
+
+            @pl.when(jnp.logical_and(z + d < n, z > 0))
+            def _():
+                to_left(z + d, h).wait_send()
+
     for j in range(1, n):
-        coarse_mass_to(pts_peer(j)).wait_send()
-        mass_to(pts_peer(j)).wait_send()
-    for d in range(1, n):
-        @pl.when(z + d < n)
-        def _():
-            sums_right(z + d).wait_send()
-
-        @pl.when(z - d >= 0)
-        def _():
-            sums_left(z - d).wait_send()
+        peer = pts_peer(j)
+        new_from(peer).wait_recv()
+        new_to(peer).wait_send()
+        piece_to(peer).wait_send()
+        coarse_mass_to(peer).wait_send()
+        mass_to(peer).wait_send()
+        sums_to(peer).wait_send()
+    for i in range(n):
+        out_coarse[i * piece : (i + 1) * piece, :] = coarse_new[i].astype(jnp.float32)
 
     for j in range(1, m):
         peer = cent_peer(j)
         result_from(peer).wait_recv()
-        out_fine[block_rows(peer), :] = arrived[peer]
+        out_fine[block_rows(peer), :] = arrived[peer].astype(jnp.float32)
     for j in range(1, m):
         result_to(cent_peer(j)).wait_send()
 
@@ -503,6 +517,7 @@
     quarter = fine_centroids.shape[1]
     slots = block_lists.shape[1]
     every_block = slots == n * own_blocks and own_blocks == m and slots <= NCOARSE
+    every_block = every_block and NCOARSE % (16 * m * n) == 0
     if not every_block:
         return general_body(
             point_codes, shard_scales, coarse_centroids, fine_centroids, block_lists, live_counts
@@ -511,34 +526,41 @@
     f32, bf16 = jnp.float32, jnp.bfloat16
     dma = pltpu.SemaphoreType.DMA
     vmem = pl.BlockSpec(memory_space=pltpu.VMEM)
+    hbm = pl.BlockSpec(memory_space=pl.ANY)
     return pl.pallas_call(
         functools.partial(kernel, n, m),
         out_shape=(
             jax.ShapeDtypeStruct((share, width), f32),
             jax.ShapeDtypeStruct((own_blocks * BLOCK, quarter), f32),
         ),
-        in_specs=[vmem] * 6,
+        in_specs=[hbm, vmem, hbm, hbm, vmem, vmem],
         out_specs=(vmem, vmem),
         scratch_shapes=[
+            pltpu.VMEM(point_codes.shape, bf16),
+            pltpu.VMEM(coarse_centroids.shape, bf16),
             pltpu.VMEM((n, BLOCK, width), bf16),
-            pltpu.VMEM((n, share, width), bf16),
-            pltpu.VMEM((n, BLOCK, width), f32),
-            pltpu.VMEM((n, BLOCK, width), bf16),
+            pltpu.VMEM((BLOCK, width), f32),
             pltpu.VMEM((n, BLOCK, width), bf16),
             pltpu.VMEM((n, BLOCK, width), bf16),
             pltpu.VMEM((slots, points), f32),
             pltpu.VMEM((NCOARSE, points), f32),
+            pltpu.VMEM((share, width), bf16),
+            pltpu.VMEM((share, width), f32),
+            pltpu.VMEM((n, share // n, width), bf16),
+            pltpu.VMEM((n, share // n, width), bf16),
             pltpu.VMEM((n, 8, 128), f32),
             pltpu.VMEM((n, 8, 128), f32),
             pltpu.VMEM((n, 8, 128), f32),
-            pltpu.VMEM((BLOCK, width), f32),
-            pltpu.VMEM((m, BLOCK, quarter), f32),
+            pltpu.VMEM((BLOCK, width), bf16),
+            pltpu.VMEM((m, BLOCK, quarter), bf16),
+            dma((3,)),
         ]
         + [dma((m,))] * 2
-        + [dma((n,))] * 13
+        + [dma((n, HALVES))] * 3
+        + [dma((n,))] * 10
         + [dma((m,))] * 2,
         compiler_params=pltpu.CompilerParams(
-            collective_id=0, has_side_effects=True, vmem_limit_bytes=40 * 1024 * 1024
+            collective_id=0, has_side_effects=True, vmem_limit_bytes=60 * 1024 * 1024
         ),
     )(
         point_codes,

time: 47.8 us -> 42.2 us (0.88)
  local copies, waits for them, and re-layouts: 5.23 us -> 2.42 us
  Pallas kernels: 41 us -> 38.3 us
    unnamed x12 -> x4, local copies, waits for them, and re-layouts: 5.23 us -> 2.42 us
    pallas_call x1, Pallas kernels: 41 us -> 38.3 us  [body(): pl.pallas_call(functools.partial(kernel, n, m), out_shape=(jax.ShapeDtype...]
where the time goes in v2:
time: 42.2 us; the launch traced here: 42 us
  Pallas kernels  38.3 us (91%)
  local copies, waits for them, and re-layouts  2.42 us (6%)
  between operations  1.29 us (3%)
    pallas_call x1, Pallas kernels, body(): pl.pallas_call(functools.partial(kernel, n, m), out_shape=(jax.ShapeDtype...  38.3 us
    unnamed x4, local copies, waits for them, and re-layouts  2.42 us

profile of v2, /device:TPU:0, one launch (start us, length us, event | category | flops | bytes accessed | tf_op | source)
XLA Modules:
  0.0 42.0 jit_solution(10510835700176375932)
XLA Ops:
  1.3 38.3 %shard_map.77 = (f32[64,1024]{1,0:T(8,128)}, f32[256,256]{1,0:T(8,128)}) custom-call(bf16[512,1024]{1,0:T(8,128)(2,1)} %codes_in.1, f32[1,2]{1,0:T(1,128)} %bitcast.3, bf16[256,1024]{1,0:T(8,128)(2,1)} %coarse_in.1, bf16[256,256]{1,0:T(8,128)(2,1)} %fine.1, s32[1,16]{1,0:T(1,128)} %lists.1, s32[1,1]{1,0:T(1,128)} %bitcast.2.counts), custom_call_target="tpu_custom_call" | custom-call | tf_op jit(solution)/shard_map/pallas_call | solution.py:530
  39.6 0.0 copy-start
  39.6 1.7 %copy.11 = f32[64,1024]{1,0:T(8,128)} copy(f32[64,1024]{1,0:T(8,128)} %get-tuple-element.4) | data formatting | bytes 524288
  41.3 0.0 copy-done
  41.3 0.7 %copy.12 = f32[256,256]{1,0:T(8,128)} copy(f32[256,256]{1,0:T(8,128)S(1)} %copy-done) | data formatting | bytes 524288
Async XLA Ops:
  39.6 1.7 %copy-start = (f32[256,256]{1,0:T(8,128)S(1)}, f32[256,256]{1,0:T(8,128)}, u32[]{:S(2)}) copy-start(f32[256,256]{1,0:T(8,128)} %get-tuple-element.5) | copy-start | bytes 786436

commit v3 on v2

--- a/solution.py
+++ b/solution.py
@@ -447,7 +447,7 @@
         def _():
             use_and_send(z + d)
 
-        if d == 1:
+        if d == max(1, n - 2):
             finish_coarse_piece()
 
     total = own_part[...] + PRIOR_MASS * rows[z].astype(jnp.float32)

time: 42.2 us -> 41.2 us (0.976)
  Pallas kernels: 38.3 us -> 37.3 us
    pallas_call x1, Pallas kernels: 38.3 us -> 37.3 us  [body(): pl.pallas_call(functools.partial(kernel, n, m), out_shape=(jax.ShapeDtype...]
where the time goes in v3:
time: 41.2 us; the launch traced here: 41 us
  Pallas kernels  37.3 us (91%)
  local copies, waits for them, and re-layouts  2.42 us (6%)
  between operations  1.29 us (3%)
    pallas_call x1, Pallas kernels, body(): pl.pallas_call(functools.partial(kernel, n, m), out_shape=(jax.ShapeDtype...  37.3 us
    unnamed x4, local copies, waits for them, and re-layouts  2.42 us

profile of v3, /device:TPU:0, one launch (start us, length us, event | category | flops | bytes accessed | tf_op | source)
XLA Modules:
  0.0 41.0 jit_solution(5665915267195600568)
XLA Ops:
  1.3 37.3 %shard_map.77 = (f32[64,1024]{1,0:T(8,128)}, f32[256,256]{1,0:T(8,128)}) custom-call(bf16[512,1024]{1,0:T(8,128)(2,1)} %codes_in.1, f32[1,2]{1,0:T(1,128)} %bitcast.3, bf16[256,1024]{1,0:T(8,128)(2,1)} %coarse_in.1, bf16[256,256]{1,0:T(8,128)(2,1)} %fine.1, s32[1,16]{1,0:T(1,128)} %lists.1, s32[1,1]{1,0:T(1,128)} %bitcast.2.counts), custom_call_target="tpu_custom_call" | custom-call | tf_op jit(solution)/shard_map/pallas_call | solution.py:530
  38.6 0.0 copy-start
  38.6 1.7 %copy.11 = f32[64,1024]{1,0:T(8,128)} copy(f32[64,1024]{1,0:T(8,128)} %get-tuple-element.4) | data formatting | bytes 524288
  40.3 0.0 copy-done
  40.3 0.7 %copy.12 = f32[256,256]{1,0:T(8,128)} copy(f32[256,256]{1,0:T(8,128)S(1)} %copy-done) | data formatting | bytes 524288
Async XLA Ops:
  38.6 1.7 %copy-start = (f32[256,256]{1,0:T(8,128)S(1)}, f32[256,256]{1,0:T(8,128)}, u32[]{:S(2)}) copy-start(f32[256,256]{1,0:T(8,128)} %get-tuple-element.5) | copy-start | bytes 786436

commit v4 on v3

--- a/solution.py
+++ b/solution.py
@@ -14,7 +14,7 @@
 
 PRIOR_MASS = 1.0
 MASK_SCORE = -1e30
-HALVES = 2
+HALVES = 4
 
 
 def joined(part, axis, combine):

time: 41.2 us -> 41.4 us (level)
  no operation moved by 1% of the time
where the time goes in v4:
time: 41.4 us; the launch traced here: 41.2 us
  Pallas kernels  37.5 us (91%)
  local copies, waits for them, and re-layouts  2.42 us (6%)
  between operations  1.29 us (3%)
    pallas_call x1, Pallas kernels, body(): pl.pallas_call(functools.partial(kernel, n, m), out_shape=(jax.ShapeDtype...  37.5 us
    unnamed x4, local copies, waits for them, and re-layouts  2.42 us

profile of v4, /device:TPU:0, one launch (start us, length us, event | category | flops | bytes accessed | tf_op | source)
XLA Modules:
  0.0 41.2 jit_solution(13739041497577323971)
XLA Ops:
  1.3 37.5 %shard_map.77 = (f32[64,1024]{1,0:T(8,128)}, f32[256,256]{1,0:T(8,128)}) custom-call(bf16[512,1024]{1,0:T(8,128)(2,1)} %codes_in.1, f32[1,2]{1,0:T(1,128)} %bitcast.3, bf16[256,1024]{1,0:T(8,128)(2,1)} %coarse_in.1, bf16[256,256]{1,0:T(8,128)(2,1)} %fine.1, s32[1,16]{1,0:T(1,128)} %lists.1, s32[1,1]{1,0:T(1,128)} %bitcast.2.counts), custom_call_target="tpu_custom_call" | custom-call | tf_op jit(solution)/shard_map/pallas_call | solution.py:530
  38.8 0.0 copy-start
  38.8 1.7 %copy.11 = f32[64,1024]{1,0:T(8,128)} copy(f32[64,1024]{1,0:T(8,128)} %get-tuple-element.4) | data formatting | bytes 524288
  40.5 0.0 copy-done
  40.5 0.7 %copy.12 = f32[256,256]{1,0:T(8,128)} copy(f32[256,256]{1,0:T(8,128)S(1)} %copy-done) | data formatting | bytes 524288
Async XLA Ops:
  38.8 1.7 %copy-start = (f32[256,256]{1,0:T(8,128)S(1)}, f32[256,256]{1,0:T(8,128)}, u32[]{:S(2)}) copy-start(f32[256,256]{1,0:T(8,128)} %get-tuple-element.5) | copy-start | bytes 786436
